TPU v7x, 32 devices: a whole 2x2x4 slice. The times are simulated.
32 devices in a mesh: group: 2 (over y), expert: 4 (over x, core), tensor: 4 (over z).
Axes of the slice: x: 2, y: 2, z: 4, core: 2. Of those that a mesh axis runs over, the one named last changes fastest.
Arguments:
- tokens: bfloat16 [256, 6144], P(('group', 'expert'), 'tensor'), parts along dimension 0, may hold values from -6 to 6
- route_experts: int32 [256, 2], P(('group', 'expert')), parts along dimension 0, may hold values from 0 to 3, all different within a row; in each aligned block of 32 rows (0 to 31, 32 to 63, ...) at most 20 rows name the same one
- route_weight_values: bfloat16 [256, 2], P(('group', 'expert')), parts along dimension 0, may hold values from 0.099609375 to 0.8984375
- cotangent: bfloat16 [256, 6144], P(('group', 'expert'), 'tensor'), parts along dimension 0, may hold values from -6 to 6
- gate_weight_frozen: bfloat16 [4, 6144, 8192], P('expert', None, 'tensor'), may hold values from -0.078125 to 0.078125
- up_weight_frozen: bfloat16 [4, 6144, 8192], P('expert', None, 'tensor'), may hold values from -0.078125 to 0.078125
- down_weight_frozen: bfloat16 [4, 8192, 6144], P('expert', 'tensor'), may hold values from -0.0625 to 0.0625
- entry_input_maps: bfloat16 [8, 2, 6144, 16], P('group', None, 'tensor'), parts along dimension 0, may hold values from -0.078125 to 0.078125
- entry_output_maps: bfloat16 [8, 2, 16, 8192], P(('group', 'expert'), None, None, 'tensor'), parts along dimension 0, may hold values from -0.29882812 to 0.29882812
- down_input_maps: bfloat16 [8, 8192, 16], P(('group', 'expert'), 'tensor'), parts along dimension 0, may hold values from -0.0625 to 0.0625
- down_output_maps: bfloat16 [8, 16, 6144], P('group', None, 'tensor'), parts along dimension 0, may hold values from -0.29882812 to 0.29882812
Outputs:
- mixed: bfloat16 [256, 6144], P(('group', 'expert'), 'tensor'), parts along dimension 0
- grad_tokens: bfloat16 [256, 6144], P(('group', 'expert'), 'tensor'), parts along dimension 0
- entry_inmaps_gradient: float32 [8, 2, 6144, 16], P('group', None, ('expert', 'tensor')), parts along dimension 0
- entry_outmaps_gradient: float32 [8, 2, 16, 8192], P(('group', 'expert'), None, None, 'tensor'), parts along dimension 0
- down_inmaps_gradient: float32 [8, 8192, 16], P(('group', 'expert'), 'tensor'), parts along dimension 0
- down_outmaps_gradient: float32 [8, 16, 6144], P('group', None, ('expert', 'tensor')), parts along dimension 0
There are 2 independent parts, one for each index of `group`. A program takes and returns all parts, laid end to end along the dimension named above; an argument that names none is the same for every part. Nothing has to cross between parts.
Inputs may be any that keep to these rules, and one draw needn't show every extreme that they name: `route_experts`: each token names 2 different experts. Among the tokens of one index of expert (aligned blocks of 32 tokens) no expert is named by more than 20 of them, and in every draw some block has an expert named by exactly 20.
All inputs are finite; a program needn't handle non-finite values.
Results may differ from a plain program's by a relative error of at most 0.006.
Values may be sent and summed in bfloat16 or wider, within the bound.
A program may use at most 192 MiB of HBM per device.

v0:
```python
import jax
import jax.numpy as jnp
from jax import lax
from jax.sharding import PartitionSpec as P

MOST = 20


adapter_scale = 2.0
exact_precision = lax.Precision.HIGHEST


def expert_forward_step(
    expert_token_rows,
    expert_gradient_rows,
    expert_gate_values,
    gate_weight_slices,
    up_weight_slices,
    down_weight_slices,
    adapter_a_in,
    entry_adapter_outmaps,
    down_adapter_inmaps,
    adapter_b_down,
):
    narrow_gate = jnp.dot(
        expert_token_rows, adapter_a_in[0], preferred_element_type=jnp.float32
    ).astype(jnp.bfloat16)
    narrow_up = jnp.dot(
        expert_token_rows, adapter_a_in[1], preferred_element_type=jnp.float32
    ).astype(jnp.bfloat16)
    gate_preactivation = jnp.dot(
        expert_token_rows, gate_weight_slices, preferred_element_type=jnp.float32
    ) + adapter_scale * jnp.dot(
        narrow_gate, entry_adapter_outmaps[0], preferred_element_type=jnp.float32
    )
    up_preactivation = jnp.dot(
        expert_token_rows, up_weight_slices, preferred_element_type=jnp.float32
    ) + adapter_scale * jnp.dot(
        narrow_up, entry_adapter_outmaps[1], preferred_element_type=jnp.float32
    )
    sigmoid_gate = jax.nn.sigmoid(gate_preactivation)
    silu_gate = gate_preactivation * sigmoid_gate
    hidden_state = (silu_gate * up_preactivation).astype(jnp.bfloat16)
    narrow_down = jnp.dot(hidden_state, down_adapter_inmaps, preferred_element_type=jnp.float32)
    down_output_maps_spread = adapter_b_down.astype(jnp.float32)
    expert_output_rows = jnp.dot(
        hidden_state, down_weight_slices, preferred_element_type=jnp.float32
    ) + adapter_scale * jnp.dot(narrow_down, down_output_maps_spread, precision=exact_precision)
    weighted = expert_gate_values * expert_output_rows
    output_gradient = (expert_gate_values * expert_gradient_rows.astype(jnp.float32)).astype(
        jnp.bfloat16
    )
    narrow_gradient = jnp.dot(output_gradient, adapter_b_down.T, preferred_element_type=jnp.float32)
    hidden_gradient = jnp.dot(
        output_gradient, down_weight_slices.T, preferred_element_type=jnp.float32
    ) + adapter_scale * jnp.dot(
        narrow_gradient, down_adapter_inmaps.astype(jnp.float32).T, precision=exact_precision
    )
    down_inmaps_gradient = adapter_scale * jnp.dot(
        hidden_state.astype(jnp.float32).T, narrow_gradient, precision=exact_precision
    )
    down_outmaps_gradient = adapter_scale * jnp.dot(
        narrow_down.T, output_gradient.astype(jnp.float32), precision=exact_precision
    )
    gate_gradient = (
        hidden_gradient
        * up_preactivation
        * sigmoid_gate
        * (1.0 + gate_preactivation * (1.0 - sigmoid_gate))
    ).astype(jnp.bfloat16)
    up_gradient = (hidden_gradient * silu_gate).astype(jnp.bfloat16)
    reverse_gate_step = jnp.dot(
        gate_gradient, entry_adapter_outmaps[0].T, preferred_element_type=jnp.float32
    )
    reverse_up_step = jnp.dot(
        up_gradient, entry_adapter_outmaps[1].T, preferred_element_type=jnp.float32
    )
    entry_outmaps_gradient = adapter_scale * jnp.stack(
        [
            jnp.dot(narrow_gate.T, gate_gradient, preferred_element_type=jnp.float32),
            jnp.dot(narrow_up.T, up_gradient, preferred_element_type=jnp.float32),
        ]
    )
    token_rows_spread = expert_token_rows.astype(jnp.float32)
    entry_inmaps_gradient = adapter_scale * jnp.stack(
        [
            jnp.dot(token_rows_spread.T, reverse_gate_step, precision=exact_precision),
            jnp.dot(token_rows_spread.T, reverse_up_step, precision=exact_precision),
        ]
    )
    entry_input_maps_spread = adapter_a_in.astype(jnp.float32)
    input_gradient = jnp.dot(
        gate_gradient, gate_weight_slices.T, preferred_element_type=jnp.float32
    ) + jnp.dot(up_gradient, up_weight_slices.T, preferred_element_type=jnp.float32)
    input_gradient = input_gradient + adapter_scale * (
        jnp.dot(reverse_gate_step, entry_input_maps_spread[0].T, precision=exact_precision)
        + jnp.dot(reverse_up_step, entry_input_maps_spread[1].T, precision=exact_precision)
    )
    return (
        weighted,
        input_gradient,
        entry_inmaps_gradient,
        entry_outmaps_gradient,
        down_inmaps_gradient,
        down_outmaps_gradient,
    )


def route_positions(route_experts, expert_number):
    flat_ids = route_experts.reshape(-1)
    expert_labels = jnp.arange(expert_number, dtype=jnp.int32)
    one_hot = (flat_ids[:, None] == expert_labels[None, :]).astype(jnp.int32)
    earlier = jnp.cumsum(one_hot, axis=0) - one_hot
    return jnp.sum(earlier * one_hot, axis=1)


def spread_slots(rows, expert_number, capacity, copy_count):
    return jnp.repeat(rows.reshape((expert_number, capacity) + rows.shape[1:]), copy_count, axis=0)


def collect_rows(back, token_hits, expert_number, copy_count, capacity):
    row_width = back.shape[2]
    merged = jnp.sum(back.reshape(expert_number, copy_count, capacity, row_width), axis=1).reshape(
        expert_number * capacity, row_width
    )
    return jnp.dot(token_hits.T, merged, precision=exact_precision)


def local(
    tokens,
    route_experts,
    route_weight_values,
    cotangent,
    gate_weight_frozen,
    up_weight_frozen,
    down_weight_frozen,
    entry_input_maps,
    entry_output_maps,
    down_input_maps,
    down_output_maps,
):
    tok_rows = tokens.shape[0]
    expert_number = entry_input_maps.shape[0]
    adapter_rank_count = entry_input_maps.shape[3]
    route_count = route_experts.shape[1]
    owner_count = lax.axis_size("expert")
    tensor_count = lax.axis_size("tensor")
    model_width = tokens.shape[1] * tensor_count
    copy_count = owner_count // expert_number
    capacity = MOST
    flat_ids = route_experts.reshape(-1)
    position = route_positions(route_experts, expert_number)
    slot_of = flat_ids * capacity + position
    slot_ids = jnp.arange(expert_number * capacity, dtype=jnp.int32)
    chosen = slot_ids[:, None] == slot_of[None, :]
    pick_route = chosen.astype(jnp.bfloat16)
    hit_counts = jnp.sum(
        chosen.reshape(expert_number * capacity, tok_rows, route_count).astype(jnp.int32), axis=2
    )
    pick_token = hit_counts.astype(jnp.bfloat16)
    token_hits = hit_counts.astype(jnp.float32)
    send_gates = jnp.dot(
        pick_route, route_weight_values.reshape(-1), preferred_element_type=jnp.float32
    ).astype(jnp.bfloat16)
    send_gates = spread_slots(send_gates, expert_number, capacity, copy_count)
    full_tokens, full_grads = (
        lax.all_gather(tokens, "tensor", axis=1, tiled=True),
        lax.all_gather(cotangent, "tensor", axis=1, tiled=True),
    )
    send_tokens = spread_slots(
        jnp.dot(pick_token, full_tokens, preferred_element_type=jnp.float32).astype(jnp.bfloat16),
        expert_number,
        capacity,
        copy_count,
    )
    send_grads = spread_slots(
        jnp.dot(pick_token, full_grads, preferred_element_type=jnp.float32).astype(jnp.bfloat16),
        expert_number,
        capacity,
        copy_count,
    )
    got_tokens, got_grads, got_gates = (
        lax.all_to_all(send_tokens, "expert", split_axis=0, concat_axis=0, tiled=True),
        lax.all_to_all(send_grads, "expert", split_axis=0, concat_axis=0, tiled=True),
        lax.all_to_all(send_gates, "expert", split_axis=0, concat_axis=0, tiled=True),
    )
    holder_index = lax.axis_index("expert") // copy_count
    entry_input_maps_local = lax.dynamic_index_in_dim(
        entry_input_maps, holder_index, 0, keepdims=False
    )
    down_output_maps_local = lax.dynamic_index_in_dim(
        down_output_maps, holder_index, 0, keepdims=False
    )
    a_in_full, b_down_full = (
        lax.all_gather(entry_input_maps_local, "tensor", axis=1, tiled=True),
        lax.all_gather(down_output_maps_local, "tensor", axis=1, tiled=True),
    )
    expert_token_rows = got_tokens.reshape(-1, model_width)
    expert_gradient_rows = got_grads.reshape(-1, model_width)
    expert_gate_values = got_gates.reshape(-1).astype(jnp.float32)[:, None]
    step_results = expert_forward_step(
        expert_token_rows,
        expert_gradient_rows,
        expert_gate_values,
        gate_weight_frozen[0],
        up_weight_frozen[0],
        down_weight_frozen[0],
        a_in_full,
        entry_output_maps[0],
        down_input_maps[0],
        b_down_full,
    )
    (
        weighted,
        input_gradient,
        entry_inmaps_gradient,
        entry_outmaps_gradient,
        down_inmaps_gradient,
        down_outmaps_gradient,
    ) = step_results
    weighted = weighted.reshape(owner_count, capacity, model_width)
    input_gradient = input_gradient.reshape(owner_count, capacity, model_width)
    back_out, back_grad = (
        lax.all_to_all(weighted, "expert", split_axis=0, concat_axis=0, tiled=True),
        lax.all_to_all(input_gradient, "expert", split_axis=0, concat_axis=0, tiled=True),
    )
    token_out = collect_rows(back_out, token_hits, expert_number, copy_count, capacity)
    token_grad = collect_rows(back_grad, token_hits, expert_number, copy_count, capacity)
    total_out, total_grad = (
        lax.psum_scatter(token_out, "tensor", scatter_dimension=1, tiled=True),
        lax.psum_scatter(token_grad, "tensor", scatter_dimension=1, tiled=True),
    )
    table_a_in = jnp.zeros((expert_number, 2, model_width, adapter_rank_count), jnp.float32)
    table_a_in = lax.dynamic_update_index_in_dim(table_a_in, entry_inmaps_gradient, holder_index, 0)
    table_b_down = jnp.zeros((expert_number, adapter_rank_count, model_width), jnp.float32)
    table_b_down = lax.dynamic_update_index_in_dim(
        table_b_down, down_outmaps_gradient, holder_index, 0
    )
    summed_a_in, summed_b_down = (
        lax.psum_scatter(table_a_in, ("expert", "tensor"), scatter_dimension=2, tiled=True),
        lax.psum_scatter(table_b_down, ("expert", "tensor"), scatter_dimension=2, tiled=True),
    )
    return (
        total_out.astype(jnp.bfloat16),
        total_grad.astype(jnp.bfloat16),
        summed_a_in,
        entry_outmaps_gradient[None],
        down_inmaps_gradient[None],
        summed_b_down,
    )


def solution(mesh):
    in_specs = (
        P(("group", "expert"), "tensor"),
        P(("group", "expert"), None),
        P(("group", "expert"), None),
        P(("group", "expert"), "tensor"),
        P("expert", None, "tensor"),
        P("expert", None, "tensor"),
        P("expert", "tensor", None),
        P("group", None, "tensor", None),
        P(("group", "expert"), None, None, "tensor"),
        P(("group", "expert"), "tensor", None),
        P("group", None, "tensor"),
    )
    out_specs = (
        P(("group", "expert"), "tensor"),
        P(("group", "expert"), "tensor"),
        P("group", None, ("expert", "tensor"), None),
        P(("group", "expert"), None, None, "tensor"),
        P(("group", "expert"), "tensor", None),
        P("group", None, ("expert", "tensor")),
    )
    return jax.shard_map(local, mesh=mesh, in_specs=in_specs, out_specs=out_specs, check_vma=False)
```

profile of v0, /device:TPU:0, one launch (start us, length us, event | category | flops | bytes accessed | tf_op | source)
XLA Modules:
  0.0 403.0 jit_solution(326399183051393087)
XLA Ops:
  7.2 0.8 copy.38
  8.1 0.8 copy.36
  9.5 0.7 all_to_all.24
  10.2 4.2 %all-to-all-start = ((bf16[4,1,20]{2,1,0:T(2,128)(2,1)}), bf16[4,1,20]{2,1,0:T(2,128)(2,1)S(1)}, u32[]{:S(2)}, u32[]{:S(2)}) async-start(bf16[4,1,20]{2,1,0:T(2,128)(2,1)} %all_to_all.24), calls=%async_computation | async-start | bytes 4096 | tf_op jit(solution)/shard_map/all_to_all | solution.py:185
  14.5 0.7 multiply_add_fusion
  15.3 15.7 %all_gather.12 = bf16[32,6144]{1,0:T(8,128)(2,1)S(1)} all-gather(bf16[32,1536]{1,0:T(8,128)(2,1)} %param.11), channel_id=1, replica_groups=mesh['group'=2,'expert'=4,'tensor'=4] {'tensor'}, dimensions={1}, use_global_device_ids=true | all-gather | bytes 491520 | tf_op jit(solution)/shard_map/all_gather | solution.py:167
  31.0 15.4 %all_gather.15 = bf16[32,6144]{1,0:T(8,128)(2,1)S(1)} all-gather(bf16[32,1536]{1,0:T(8,128)(2,1)} %param.14), channel_id=1, replica_groups=mesh['group'=2,'expert'=4,'tensor'=4] {'tensor'}, dimensions={1}, use_global_device_ids=true | all-gather | bytes 491520 | tf_op jit(solution)/shard_map/all_gather | solution.py:168
  46.4 0.4 convolution_convert_fusion
  46.8 1.1 reshape_broadcast_in_dim_reshape.8
  48.0 0.4 convolution_convert_fusion.1
  48.4 1.2 reshape_broadcast_in_dim_reshape.7
  49.6 3.7 all-to-all-start.1
  53.2 0.8 constant_dynamic-slice_fusion
  54.1 14.4 %all-gather.1 = bf16[1,16,6144]{2,1,0:T(8,128)(2,1)} all-gather(bf16[1,16,1536]{2,1,0:T(8,128)(2,1)S(1)} %constant_dynamic-slice_fusion), channel_id=3, replica_groups=mesh['group'=2,'expert'=4,'tensor'=4] {'tensor'}, dimensions={2}, use_global_device_ids=true | all-gather | bytes 245760 | tf_op jit(solution)/shard_map/all_gather | solution.py:196
  68.4 15.2 %all-gather = bf16[1,2,6144,16]{2,3,1,0:T(8,128)(2,1)S(1)} all-gather(bf16[1,2,1536,16]{2,3,1,0:T(8,128)(2,1)S(1)} %constant_dynamic-slice_fusion.1), channel_id=2, replica_groups=mesh['group'=2,'expert'=4,'tensor'=4] {'tensor'}, dimensions={2}, use_global_device_ids=true | all-gather | bytes 491520 | tf_op jit(solution)/shard_map/all_gather | solution.py:195
  83.6 0.6 reshape.154
  84.3 1.0 copy-done.4
  85.3 3.7 all-to-all-start.3
  89.0 1.4 reshape.149
  90.4 11.3 %fusion.6 = f32[80,2048]{1,0:T(8,128)} fusion(bf16[80,6144]{1,0:T(8,128)(2,1)S(1)} %reshape.149, bf16[1,6144,2048]{2,1,0:T(8,128)(2,1)} %param.16), kind=kOutput, calls=%fused_computation.6 | convolution fusion | flops 2013265920 | bytes 26804224 | tf_op jit(solution)/shard_map/dot_general | solution.py:36
  101.7 11.3 %fusion.10 = f32[80,2048]{1,0:T(8,128)} fusion(bf16[80,6144]{1,0:T(8,128)(2,1)S(1)} %reshape.149, bf16[1,6144,2048]{2,1,0:T(8,128)(2,1)} %param.15), kind=kOutput, calls=%fused_computation.10 | convolution fusion | flops 2013265920 | bytes 26804224 | tf_op jit(solution)/shard_map/dot_general | solution.py:31
  113.0 1.0 convolution_convert_fusion.2
  113.9 1.0 convolution_convert_fusion.3
  114.9 1.4 multiply_convert_fusion
  116.3 1.4 convert_element_type.99
  117.7 13.3 %fusion = f32[80,2048]{1,0:T(8,128)} fusion(bf16[80,6144]{1,0:T(8,128)(2,1)S(1)} %convert_element_type.99, bf16[1,2048,6144]{2,1,0:T(8,128)(2,1)} %param.17), kind=kOutput, calls=%fused_computation | convolution fusion | flops 2013265920 | bytes 26804224 | tf_op jit(solution)/shard_map/dot_general | solution.py:54
  131.1 1.1 fusion.22
  132.2 1.4 reshape.156
  133.7 0.4 fusion.28
  134.1 0.6 copy-done.17
  134.7 0.5 fusion.21
  135.2 1.4 multiply_convert_fusion.3
  136.6 0.8 fusion.35
  137.4 13.7 %fusion.4 = f32[80,6144]{1,0:T(8,128)} fusion(bf16[80,2048]{1,0:T(8,128)(2,1)S(1)} %get-tuple-element.7, bf16[1,6144,2048]{2,1,0:T(8,128)(2,1)} %param.16), kind=kOutput, calls=%fused_computation.4 | convolution fusion | flops 2013265920 | bytes 27459584 | tf_op jit(solution)/shard_map/dot_general | solution.py:94
  151.1 1.2 fusion.33
  152.3 10.8 %fusion.2 = f32[80,6144]{1,0:T(8,128)S(1)} fusion(bf16[80,2048]{1,0:T(8,128)(2,1)} %get-tuple-element.8, bf16[1,2048,6144]{2,1,0:T(8,128)(2,1)} %param.17), kind=kOutput, calls=%fused_computation.2 | convolution fusion | flops 2013265920 | bytes 27459584 | tf_op jit(solution)/shard_map/dot_general | solution.py:46
  163.4 2.4 fusion.15
  165.8 2.7 reshape.150
  168.5 4.5 %all-to-all-start.2 = ((f32[4,20,6144]{2,1,0:T(8,128)}), f32[4,20,6144]{2,1,0:T(8,128)}, u32[]{:S(2)}, u32[]{:S(2)}) async-start(f32[4,20,6144]{2,1,0:T(8,128)} %reshape.150), calls=%async_computation.2 | async-start | bytes 4718592 | tf_op jit(solution)/shard_map/all_to_all | solution.py:224
  173.0 3.2 fusion.31
  176.2 14.5 %fusion.16 = f32[80,6144]{1,0:T(8,128)} fusion(f32[80,6144]{1,0:T(8,128)} %fusion.4, bf16[80,2048]{1,0:T(8,128)(2,1)S(1)} %copy-done.6, bf16[1,6144,2048]{2,1,0:T(8,128)(2,1)} %param.15), kind=kOutput, calls=%fused_computation.18 | convolution fusion | flops 2013757440 | bytes 29425664 | tf_op jit(solution)/shard_map/dot_general | solution.py:92
  190.7 4.6 %fusion.13 = f32[80,6144]{1,0:T(8,128)} fusion(f32[80,6144]{1,0:T(8,128)} %fusion.16, f32[80,6144]{1,0:T(8,128)} %fusion.31, f32[80,16]{0,1:T(8,128)S(1)} %copy-done.19, bf16[1,2,6144,16]{2,3,1,0:T(8,128)(2,1)} %copy-done.7), kind=kOutput, calls=%fused_computation.14 | convolution fusion | flops 95846400 | bytes 6099968 | tf_op jit(solution)/shard_map/dot_general | solution.py:97
  195.3 2.8 reshape.152
  198.1 3.5 all-to-all-done.2
  201.6 4.5 %all-to-all-start.4 = ((f32[4,20,6144]{2,1,0:T(8,128)}), f32[4,20,6144]{2,1,0:T(8,128)}, u32[]{:S(2)}, u32[]{:S(2)}) async-start(f32[4,20,6144]{2,1,0:T(8,128)} %reshape.152), calls=%async_computation.5 | async-start | bytes 4718592 | tf_op jit(solution)/shard_map/all_to_all | solution.py:225
  206.1 2.7 reshape.151
  208.9 3.5 fusion.49
  212.4 22.2 %all-to-all-done.4 = f32[4,20,6144]{2,1,0:T(8,128)} async-done(((f32[4,20,6144]{2,1,0:T(8,128)}), f32[4,20,6144]{2,1,0:T(8,128)}, u32[]{:S(2)}, u32[]{:S(2)}) %all-to-all-start.4) | async-done | bytes 1966112 | tf_op jit(solution)/shard_map/all_to_all | solution.py:225
  234.7 2.7 reshape.153
  237.4 3.5 fusion.47
  241.0 1.3 broadcast_in_dim.22
  242.3 1.3 fusion.20
  243.7 0.5 convolution_bitcast_fusion
  244.3 0.5 convolution_bitcast_fusion.1
  245.2 1.6 copy-done.2
  246.8 1.2 convolution_bitcast_fusion.3
  248.0 1.1 convolution_bitcast_fusion.2
  249.2 1.9 fusion.24
  251.0 0.7 maximum_multiply_fusion.1
  251.8 1.6 convert_element_type.93
  253.3 10.3 %reduce-scatter.7.cloned.1.call-done = f32[32,1536]{1,0:T(8,128)} async-done(((f32[32,6144]{1,0:T(8,128)}), f32[32,1536]{1,0:T(8,128)}) %reduce-scatter.7.cloned.1.call-update) | async-done | bytes 196624 | tf_op jit(solution)/shard_map/reduce_scatter | solution.py:231
  263.6 1.6 convert_element_type.105
  265.2 61.4 %reduce-scatter.11.cloned.1.call-done = f32[4,16,384]{2,1,0:T(8,128)} async-done(((f32[4,16,6144]{2,1,0:T(8,128)}), f32[4,16,384]{2,1,0:T(8,128)}) %reduce-scatter.11.cloned.1.call-update) | async-done | bytes 98320 | tf_op jit(solution)/shard_map/reduce_scatter | solution.py:241
  326.6 69.9 %reduce-scatter.9.cloned.1.call-done = f32[4,2,384,16]{2,3,1,0:T(8,128)} async-done(((f32[4,2,6144,16]{2,3,1,0:T(8,128)}), f32[4,2,384,16]{2,3,1,0:T(8,128)}) %reduce-scatter.9.cloned.1.call-update) | async-done | bytes 196624 | tf_op jit(solution)/shard_map/reduce_scatter | solution.py:240
  (85 shorter events, 2.1 us)
Async XLA Ops:
  7.2 61.3 %copy-start = (bf16[4,2,1536,16]{2,3,1,0:T(8,128)(2,1)S(1)}, bf16[4,2,1536,16]{2,3,1,0:T(8,128)(2,1)}, u32[]{:S(2)}) copy-start(bf16[4,2,1536,16]{2,3,1,0:T(8,128)(2,1)} %param.18) | copy-start | bytes 1179652
  10.2 39.4 %all-to-all-start = ((bf16[4,1,20]{2,1,0:T(2,128)(2,1)}), bf16[4,1,20]{2,1,0:T(2,128)(2,1)S(1)}, u32[]{:S(2)}, u32[]{:S(2)}) async-start(bf16[4,1,20]{2,1,0:T(2,128)(2,1)} %all_to_all.24), calls=%async_computation | async-start | bytes 4096 | tf_op jit(solution)/shard_map/all_to_all | solution.py:185
  49.6 34.7 %all-to-all-start.1 = ((bf16[4,20,6144]{2,1,0:T(8,128)(2,1)}), bf16[4,20,6144]{2,1,0:T(8,128)(2,1)S(1)}, u32[]{:S(2)}, u32[]{:S(2)}) async-start(bf16[4,20,6144]{2,1,0:T(8,128)(2,1)} %reshape_broadcast_in_dim_reshape.7), calls=%async_computation.1 | async-start | bytes 2359296 | tf_op jit(solution)/shard_map/all_to_all | solution.py:183
  83.6 30.3 %copy-start.7 = (bf16[1,2,6144,16]{2,3,1,0:T(8,128)(2,1)}, bf16[1,2,6144,16]{2,3,1,0:T(8,128)(2,1)S(1)}, u32[]{:S(2)}) copy-start(bf16[1,2,6144,16]{2,3,1,0:T(8,128)(2,1)S(1)} %all-gather) | copy-start | bytes 1179652
  84.3 1.0 copy-start.4
  85.3 29.6 %all-to-all-start.3 = ((bf16[4,20,6144]{2,1,0:T(8,128)(2,1)}), bf16[4,20,6144]{2,1,0:T(8,128)(2,1)S(1)}, u32[]{:S(2)}, u32[]{:S(2)}) async-start(bf16[4,20,6144]{2,1,0:T(8,128)(2,1)} %reshape_broadcast_in_dim_reshape.8), calls=%async_computation.4 | async-start | bytes 2359296 | tf_op jit(solution)/shard_map/all_to_all | solution.py:184
  114.9 2.8 copy-start.3
  117.7 13.4 %copy-start.8 = (f32[80,2048]{1,0:T(8,128)S(1)}, f32[80,2048]{1,0:T(8,128)}, u32[]{:S(2)}) copy-start(f32[80,2048]{1,0:T(8,128)} %fusion.6) | copy-start | bytes 1966084
  117.7 13.4 %copy-start.13 = (bf16[1,2,16,2048]{3,2,1,0:T(8,128)(2,1)S(1)}, bf16[1,2,16,2048]{3,2,1,0:T(8,128)(2,1)}, u32[]{:S(2)}) copy-start(bf16[1,2,16,2048]{3,2,1,0:T(8,128)(2,1)} %param.19) | copy-start | bytes 393220
  117.7 13.4 %copy-start.24 = (bf16[80,16]{0,1:T(8,128)(2,1)S(1)}, bf16[80,16]{0,1:T(8,128)(2,1)}, u32[]{:S(2)}) copy-start(bf16[80,16]{0,1:T(8,128)(2,1)} %convolution_convert_fusion.2) | copy-start | bytes 7684
  131.1 2.5 copy-start.10
  131.1 2.5 copy-start.28
  132.2 2.5 copy-start.16
  133.6 1.1 copy-start.9
  133.6 1.6 copy-start.11
  133.6 1.6 copy-start.12
  133.7 1.6 copy-start.14
  133.7 1.6 copy-start.26
  134.1 0.6 copy-start.17
  136.6 14.5 %copy-start.5 = (bf16[80,2048]{1,0:T(8,128)(2,1)}, bf16[80,2048]{1,0:T(8,128)(2,1)S(1)}, u32[]{:S(2)}) copy-start(bf16[80,2048]{1,0:T(8,128)(2,1)S(1)} %get-tuple-element.7) | copy-start | bytes 983044
  152.3 11.0 %copy-start.22 = (f32[80,16]{0,1:T(8,128)}, f32[80,16]{0,1:T(8,128)S(1)}, u32[]{:S(2)}) copy-start(f32[80,16]{0,1:T(8,128)S(1)} %fusion.33) | copy-start | bytes 15364
  152.3 10.8 %copy-start.6 = (bf16[80,2048]{1,0:T(8,128)(2,1)S(1)}, bf16[80,2048]{1,0:T(8,128)(2,1)}, u32[]{:S(2)}) copy-start(bf16[80,2048]{1,0:T(8,128)(2,1)} %get-tuple-element.6) | copy-start | bytes 983044
  152.3 10.8 %copy-start.15 = (bf16[1,2,16,2048]{3,2,1,0:T(8,128)(2,1)S(1)}, bf16[1,2,16,2048]{3,2,1,0:T(8,128)(2,1)}, u32[]{:S(2)}) copy-start(bf16[1,2,16,2048]{3,2,1,0:T(8,128)(2,1)} %param.19) | copy-start | bytes 393220
  152.3 11.0 %copy-start.29 = (f32[80]{0:T(128)S(1)}, f32[80]{0:T(128)}, u32[]{:S(2)}) copy-start(f32[80]{0:T(128)} %reshape.154) | copy-start | bytes 964
  163.3 9.7 %copy-start.20 = (f32[80,16]{0,1:T(8,128)}, f32[80,16]{0,1:T(8,128)S(1)}, u32[]{:S(2)}) copy-start(f32[80,16]{0,1:T(8,128)S(1)} %fusion.38) | copy-start | bytes 15364
  168.5 33.1 %all-to-all-start.2 = ((f32[4,20,6144]{2,1,0:T(8,128)}), f32[4,20,6144]{2,1,0:T(8,128)}, u32[]{:S(2)}, u32[]{:S(2)}) async-start(f32[4,20,6144]{2,1,0:T(8,128)} %reshape.150), calls=%async_computation.2 | async-start | bytes 4718592 | tf_op jit(solution)/shard_map/all_to_all | solution.py:224
  176.2 14.5 %copy-start.19 = (f32[80,16]{0,1:T(8,128)S(1)}, f32[80,16]{0,1:T(8,128)}, u32[]{:S(2)}) copy-start(f32[80,16]{0,1:T(8,128)} %fusion.35) | copy-start | bytes 15364
  201.6 33.1 %all-to-all-start.4 = ((f32[4,20,6144]{2,1,0:T(8,128)}), f32[4,20,6144]{2,1,0:T(8,128)}, u32[]{:S(2)}, u32[]{:S(2)}) async-start(f32[4,20,6144]{2,1,0:T(8,128)} %reshape.152), calls=%async_computation.5 | async-start | bytes 4718592 | tf_op jit(solution)/shard_map/all_to_all | solution.py:225
  206.1 45.7 %reduce-scatter.5.cloned.1.call-start = ((), (), s32[]{:S(2)}) async-start(), calls=%async_computation.9 | async-start | bytes 983040 | tf_op jit(solution)/shard_map/reduce_scatter | solution.py:230
  212.4 51.2 %reduce-scatter.7.cloned.1.call-start = ((), (), s32[]{:S(2)}) async-start(), calls=%async_computation.10 | async-start | bytes 983040 | tf_op jit(solution)/shard_map/reduce_scatter | solution.py:231
  237.4 4.9 %copy-start.23 = (f32[80,16]{0,1:T(8,128)S(1)}, f32[80,16]{0,1:T(8,128)}, u32[]{:S(2)}) copy-start(f32[80,16]{0,1:T(8,128)} %copy-done.22) | copy-start | bytes 15364
  240.9 85.7 %reduce-scatter.11.cloned.1.call-start = ((), (), s32[]{:S(2)}) async-start(), calls=%async_computation.12 | async-start | bytes 1671168 | tf_op jit(solution)/shard_map/reduce_scatter | solution.py:241
  243.6 0.7 copy-start.21
  243.6 152.9 %reduce-scatter.9.cloned.1.call-start = ((), (), s32[]{:S(2)}) async-start(), calls=%async_computation.11 | async-start | bytes 3342336 | tf_op jit(solution)/shard_map/reduce_scatter | solution.py:240
  245.2 1.6 copy-start.2
  245.2 1.6 copy-start.27
  245.2 2.8 copy-start.25
  245.2 4.0 copy-start.18
  246.8 149.7 %copy-start.1 = (bf16[4,2,1536,16]{2,3,1,0:T(8,128)(2,1)S(1)}, bf16[4,2,1536,16]{2,3,1,0:T(8,128)(2,1)}, u32[]{:S(2)}) copy-start(bf16[4,2,1536,16]{2,3,1,0:T(8,128)(2,1)} %param.18) | copy-start | bytes 1179652
Sparse Core Ops, SparseCore 0:
  212.5 23.8 reduce-scatter.4
  241.1 22.5 reduce-scatter.6
  267.9 58.6 reduce-scatter.10
  331.3 65.1 reduce-scatter.8
where the time goes:
time: 404 us; the launch traced here: 403 us
  waiting for transfers between devices  167 us (41%)
  matrix products  107 us (26%)
  blocking collectives  60.6 us (15%)
  local copies, waits for them, and re-layouts  26.6 us (7%)
  starting transfers between devices  20.8 us (5%)
  between operations  14.2 us (4%)
  other arithmetic  6.47 us (2%)
    reduce_scatter x1, waiting for transfers between devices, local(): lax.psum_scatter(table_a_in, ('expert', 'tensor'), scatter_dimension=2, t...  69.9 us
    reduce_scatter x1, waiting for transfers between devices, local(): lax.psum_scatter(table_b_down, ('expert', 'tensor'), scatter_dimension=2,...  61.4 us
    all_to_all x1, waiting for transfers between devices, local(): lax.all_to_all(input_gradient, 'expert', split_axis=0, concat_axis=0, til...  22.2 us
    all_gather x1, blocking collectives, local(): lax.all_gather(tokens, 'tensor', axis=1, tiled=True)  15.7 us
    all_gather x1, blocking collectives, local(): lax.all_gather(cotangent, 'tensor', axis=1, tiled=True)  15.4 us
    all_gather x1, blocking collectives, local(): lax.all_gather(entry_input_maps_local, 'tensor', axis=1, tiled=True)  15.2 us
    dot_general x1, matrix products, expert_forward_step(): jnp.dot(gate_gradient, gate_weight_slices.T, preferred_element_type=jnp.f...  14.5 us
    all_gather x1, blocking collectives, local(): lax.all_gather(down_output_maps_local, 'tensor', axis=1, tiled=True)  14.4 us
  transfers between devices with their start and end apart: 9, of which 5 were waited for; matrix products, arithmetic and copies ran while one was open for 20% of the time, Pallas kernels for 0%

commit v1 on v0

--- a/solution.py
+++ b/solution.py
@@ -1,6 +1,10 @@
+import functools
+
 import jax
 import jax.numpy as jnp
 from jax import lax
+from jax.experimental import pallas as pl
+from jax.experimental.pallas import tpu as pltpu
 from jax.sharding import PartitionSpec as P
 
 MOST = 20
@@ -250,6 +254,364 @@
     )
 
 
+BF = jnp.bfloat16
+F32 = jnp.float32
+MESH = pl.DeviceIdType.MESH
+BLOCK = 256
+SLOTS = 4
+
+
+def dot_nn(a, b):
+    return jnp.dot(a, b, preferred_element_type=F32)
+
+
+def dot_nt(a, b):
+    return lax.dot_general(a, b, (((1,), (1,)), ((), ())), preferred_element_type=F32)
+
+
+def dot_exact(a, b):
+    return jnp.dot(a, b, preferred_element_type=F32, precision=exact_precision)
+
+
+def fused_kernel(
+    n_tensor,
+    tok_ref, cot_ref, gates_ref, at_ref, bd_ref, bin_ref, adt_ref, wg_ref, wu_ref, wd_ref,
+    mixed_ref, grad_ref, ein_ref, eout_ref, din_ref, dout_ref,
+    xy, small, gmat, sel_ref, selt_ref, acc, tacc, tz, ts, te, tvz, tvzt,
+    wg_buf, wu_buf, wd_buf, s1, r1, s2, r2, s3, r3, keep,
+    wsem, gz_s, gz_r, gx_s, gx_r, gs_s, gs_r, gf_s, gf_r,
+    tz_s, tz_r, te_s, te_r, c1_s, c1_r, c2_s, c2_r, c3_s, c3_r,
+):
+    e = lax.axis_index("expert")
+    t = lax.axis_index("tensor")
+    n = n_tensor
+    tr, f = tok_ref.shape
+    rows, width = gmat.shape
+    units = adt_ref.shape[1]
+    blocks = units // BLOCK
+    xi, ci = e // 2, e % 2
+    sib = 2 * xi + (1 - ci)
+    xc = 2 * (1 - xi) + ci
+    diag = 2 * (1 - xi) + (1 - ci)
+
+    def z_to(i):
+        return lax.rem(t + i, n)
+
+    def z_from(i):
+        return lax.rem(t - i + n, n)
+
+    def remote(src, dst, ss, rs, pe, pt):
+        return pltpu.make_async_remote_copy(
+            src_ref=src, dst_ref=dst, send_sem=ss, recv_sem=rs,
+            device_id={"expert": pe, "tensor": pt}, device_id_type=MESH,
+        )
+
+    def weight_copies(j, slot):
+        cols = pl.ds(pl.multiple_of(j * BLOCK, BLOCK), BLOCK)
+        return (
+            pltpu.make_async_copy(wg_ref.at[0, :, cols], wg_buf.at[slot], wsem.at[0, slot]),
+            pltpu.make_async_copy(wu_ref.at[0, :, cols], wu_buf.at[slot], wsem.at[1, slot]),
+            pltpu.make_async_copy(wd_ref.at[0, cols, :], wd_buf.at[slot], wsem.at[2, slot]),
+        )
+
+    barrier = pltpu.get_barrier_semaphore()
+    for i in range(1, n):
+        pl.semaphore_signal(
+            barrier, inc=1, device_id={"expert": e, "tensor": z_to(i)}, device_id_type=MESH
+        )
+    for j in range(1, 4):
+        pl.semaphore_signal(
+            barrier, inc=1, device_id={"expert": lax.rem(e + j, 4), "tensor": t},
+            device_id_type=MESH,
+        )
+
+    def row_ds(o):
+        return pl.ds(pl.multiple_of(o * tr, tr), tr)
+
+    def col_ds(q):
+        return pl.ds(pl.multiple_of(q * f, f), f)
+
+    def part(k, oe, ot):
+        if k == 0:
+            return xy.at[:, row_ds(oe), col_ds(ot)]
+        return small.at[ot, row_ds(oe), :]
+
+    xy[0, row_ds(e), col_ds(t)] = tok_ref[...]
+    xy[1, row_ds(e), col_ds(t)] = cot_ref[...]
+    pl.semaphore_wait(barrier, n - 1 + 3)
+
+    sends = []
+
+    def start(copy):
+        copy.start()
+        sends.append(copy)
+
+    def z_copy(k, i):
+        return remote(part(k, e, t), part(k, e, t), gz_s.at[k, i], gz_r.at[k, i], e, z_to(i))
+
+    def x_copy(k, i):
+        b = part(k, e, z_from(i))
+        return remote(b, b, gx_s.at[k, i], gx_r.at[k, i], xc, t)
+
+    def sib_copy(k, i):
+        b = part(k, e, z_from(i))
+        return remote(b, b, gs_s.at[k, i], gs_r.at[k, i], sib, t)
+
+    def fwd_copy(k, i):
+        b = part(k, xc, z_from(i))
+        return remote(b, b, gf_s.at[k, i], gf_r.at[k, i], sib, t)
+
+    def landed(k, oe, ot, rs):
+        b = part(k, oe, ot)
+        remote(b, b, rs, rs, sib, t).wait_recv()
+
+    for i in range(1, n):
+        start(z_copy(0, i))
+    start(x_copy(0, 0))
+    start(sib_copy(0, 0))
+    for j in range(min(SLOTS, blocks)):
+        for copy in weight_copies(j, j):
+            copy.start()
+
+    low = dot_nt(tok_ref[...], at_ref[...])
+    yb = dot_nt(cot_ref[...], bd_ref[...])
+    gd = gates_ref[...]
+    rank = bd_ref.shape[0] // 4
+    lane = lax.broadcasted_iota(jnp.int32, yb.shape, 1) // rank
+    scale = jnp.zeros_like(yb)
+    for j in range(4):
+        scale = jnp.where(lane == j, gd[:, j : j + 1], scale)
+    small[t, row_ds(e), 0:128] = low
+    small[t, row_ds(e), 128:256] = jnp.concatenate([yb * scale, gd], axis=1)
+    for i in range(1, n):
+        start(z_copy(1, i))
+    start(x_copy(1, 0))
+    start(sib_copy(1, 0))
+    for i in range(1, n + 1):
+        if i < n:
+            for k in range(2):
+                landed(k, e, z_from(i), gz_r.at[k, i])
+                start(x_copy(k, i))
+                start(sib_copy(k, i))
+        for k in range(2):
+            landed(k, xc, z_from(i - 1), gx_r.at[k, i - 1])
+            start(fwd_copy(k, i - 1))
+    for i in range(n):
+        for k in range(2):
+            landed(k, sib, z_from(i), gs_r.at[k, i])
+            landed(k, diag, z_from(i), gf_r.at[k, i])
+
+    total = small[0]
+    for i in range(1, n):
+        total = total + small[i]
+    ri = lax.broadcasted_iota(jnp.int32, (256, 128), 0)
+    rj = lax.broadcasted_iota(jnp.int32, (256, 128), 1)
+    hit = (rj < 32) & (ri == e * 32 + rj)
+    hit = hit | ((rj >= 32) & (rj < 48) & (ri == 128 + e * 16 + rj - 32))
+    hit = hit | ((rj == 48) & (ri == 192 + e))
+    picked = dot_exact(total, hit.astype(F32))
+    pj = lax.broadcasted_iota(jnp.int32, picked.shape, 1)
+    picked = jnp.where(pj == 48, picked * (1.0 / n), picked)
+    sel_ref[...] = picked
+    selt_ref[...] = picked.T
+    gcol = picked[:, 48:49]
+    for q in range(n):
+        c = slice(q * f, (q + 1) * f)
+        gmat[:, c] = (gcol * xy[1, :, c].astype(F32)).astype(BF)
+    acc[...] = jnp.zeros_like(acc)
+    tacc[...] = jnp.zeros_like(tacc)
+
+    def body(j, carry):
+        slot = lax.rem(j, SLOTS)
+        cg, cu, cd = weight_copies(j, slot)
+        cg.wait()
+        cu.wait()
+        cd.wait()
+        cols = pl.ds(pl.multiple_of(j * BLOCK, BLOCK), BLOCK)
+        bin0, bin1 = bin_ref[0:16, cols], bin_ref[16:32, cols]
+        adt = adt_ref[:, cols]
+        sel = sel_ref[...]
+        l0, l1, qn = sel[:, 0:16].astype(BF), sel[:, 16:32].astype(BF), sel[:, 32:48].astype(BF)
+        selt = selt_ref[0:48, :].astype(BF)
+        x = xy[0]
+        p = dot_nn(x, wg_buf[slot]) + adapter_scale * dot_nn(l0, bin0)
+        u = dot_nn(x, wu_buf[slot]) + adapter_scale * dot_nn(l1, bin1)
+        ee = dot_nt(gmat[...], wd_buf[slot]) + adapter_scale * dot_nn(qn, adt)
+        sig = jax.nn.sigmoid(p)
+        silu = p * sig
+        h = (silu * u).astype(BF)
+        dg = (ee * u * sig * (1.0 + p * (1.0 - sig))).astype(BF)
+        du = (ee * silu).astype(BF)
+        eout_ref[0:16, cols] = adapter_scale * dot_nn(selt[0:16], dg)
+        eout_ref[16:32, cols] = adapter_scale * dot_nn(selt[16:32], du)
+        din_ref[:, cols] = adapter_scale * dot_nn(selt[32:48], h)
+        tacc[0:16, :] += dot_nt(bin0, dg)
+        tacc[16:32, :] += dot_nt(bin1, du)
+        tacc[32:48, :] += dot_nt(adt, h)
+        for q in range(n):
+            c = slice(q * f, (q + 1) * f)
+            acc[0, :, c] += dot_nn(h, wd_buf[slot, :, c])
+            acc[1, :, c] += dot_nt(dg, wg_buf[slot, c, :]) + dot_nt(du, wu_buf[slot, c, :])
+
+        @pl.when(j + SLOTS < blocks)
+        def _():
+            for copy in weight_copies(j + SLOTS, slot):
+                copy.start()
+
+        return carry
+
+    lax.fori_loop(0, blocks, body, 0)
+
+    def mine(a, o, q):
+        v = acc[a, row_ds(o), col_ds(q)]
+        return v * sel_ref[row_ds(o), 48:49] if a == 0 else v
+
+    def order(i):
+        return z_to(i + 1) if i + 1 < n else t
+
+    for i in range(n):
+        q = order(i)
+        for a in range(2):
+            s1[i, 0, a] = mine(a, diag, q).astype(BF)
+            s1[i, 1, a] = mine(a, sib, q).astype(BF)
+        start(remote(s1.at[i], r1.at[i], c1_s.at[i], c1_r.at[i], sib, t))
+    tacc[32:48, :] = tacc[32:48, :] * selt_ref[48:49, :]
+    for i in range(1, n):
+        start(remote(tacc, tz.at[i], tz_s.at[i], tz_r.at[i], e, z_to(i)))
+    for i in range(n):
+        q = order(i)
+        remote(s1.at[i], r1.at[i], c1_s.at[i], c1_r.at[i], sib, t).wait_recv()
+        for a in range(2):
+            s2[i, a] = (mine(a, xc, q) + r1[i, 0, a].astype(F32)).astype(BF)
+        start(remote(s2.at[i], r2.at[i], c2_s.at[i], c2_r.at[i], xc, t))
+    t_sum = tacc[...]
+    for i in range(1, n):
+        remote(tacc, tz.at[i], tz_s.at[i], tz_r.at[i], e, z_to(i)).wait_recv()
+        t_sum = t_sum + tz[i]
+    ts[...] = t_sum
+    for j in range(1, 4):
+        start(remote(ts, te.at[j], te_s.at[j], te_r.at[j], lax.rem(e + j, 4), t))
+    for i in range(n):
+        q = order(i)
+        remote(s2.at[i], r2.at[i], c2_s.at[i], c2_r.at[i], xc, t).wait_recv()
+        for a in range(2):
+            v = mine(a, e, q) + r1[i, 1, a].astype(F32) + r2[i, a].astype(F32)
+            if i + 1 < n:
+                s3[i, a] = v.astype(BF)
+            else:
+                keep[a] = v
+        if i + 1 < n:
+            start(remote(s3.at[i], r3.at[i], c3_s.at[i], c3_r.at[i], e, q))
+
+    def place(src, v):
+        tvz[pl.ds(pl.multiple_of(src * 32, 32), 32), :] = v[0:32]
+        tvz[pl.ds(pl.multiple_of(128 + src * 16, 16), 16), :] = v[32:48]
+
+    place(e, t_sum)
+    for j in range(1, 4):
+        remote(ts, te.at[j], te_s.at[j], te_r.at[j], lax.rem(e + j, 4), t).wait_recv()
+        place(lax.rem(e - j + 4, 4), te[j])
+    piece = width // (4 * n)
+    cols = pl.ds(pl.multiple_of((e * n + t) * piece, piece), piece)
+    ein_ref[...] = adapter_scale * dot_exact(tvz[0:128, :], xy[0, :, cols].astype(F32))
+    dout_ref[...] = adapter_scale * dot_exact(tvz[128:192, :], xy[1, :, cols].astype(F32))
+    tvzt[...] = tvz[...].T
+    own = tvzt[row_ds(e), :]
+    add_out = dot_exact(own[:, 128:192], bd_ref[...].astype(F32))
+    add_grad = dot_exact(own[:, 0:128], at_ref[...].astype(F32))
+    keep[0] = keep[0] + adapter_scale * add_out
+    keep[1] = keep[1] + adapter_scale * add_grad
+    for i in range(n - 1):
+        remote(s3.at[i], r3.at[i], c3_s.at[i], c3_r.at[i], e, z_to(i + 1)).wait_recv()
+        for a in range(2):
+            keep[a] = keep[a] + r3[i, a].astype(F32)
+    mixed_ref[...] = keep[0].astype(BF)
+    grad_ref[...] = keep[1].astype(BF)
+    for copy in sends:
+        copy.wait_send()
+
+
+def fused(
+    tokens, route_experts, route_weight_values, cotangent,
+    gate_weight_frozen, up_weight_frozen, down_weight_frozen,
+    entry_input_maps, entry_output_maps, down_input_maps, down_output_maps,
+):
+    n = lax.axis_size("tensor")
+    tr, f = tokens.shape
+    width, rows = f * n, tr * 4
+    units = down_weight_frozen.shape[1]
+    labels = jnp.arange(64, dtype=jnp.int32)
+    gates = jnp.sum(
+        jnp.where(
+            route_experts[:, :, None] == labels[None, None, :],
+            route_weight_values.astype(F32)[:, :, None],
+            0.0,
+        ),
+        axis=1,
+    )
+    at = jnp.swapaxes(entry_input_maps, 2, 3).reshape(128, f)
+    bd = down_output_maps.reshape(64, f)
+    bins = entry_output_maps.reshape(32, units)
+    adt = down_input_maps[0].T
+    piece = width // (4 * n)
+    vm = pl.BlockSpec(memory_space=pltpu.VMEM)
+    anym = pl.BlockSpec(memory_space=pl.ANY)
+    sds = jax.ShapeDtypeStruct
+    dma = pltpu.SemaphoreType.DMA
+    mixed, grad, ein, eout, din, dout = pl.pallas_call(
+        functools.partial(fused_kernel, n),
+        out_shape=(
+            sds((tr, f), BF), sds((tr, f), BF), sds((128, piece), F32),
+            sds((32, units), F32), sds((16, units), F32), sds((64, piece), F32),
+        ),
+        in_specs=[vm] * 7 + [anym] * 3,
+        out_specs=(vm,) * 6,
+        scratch_shapes=[
+            pltpu.VMEM((2, rows, width), BF),
+            pltpu.VMEM((n, rows, 256), F32),
+            pltpu.VMEM((rows, width), BF),
+            pltpu.VMEM((rows, 128), F32),
+            pltpu.VMEM((128, rows), F32),
+            pltpu.VMEM((2, rows, width), F32),
+            pltpu.VMEM((48, rows), F32),
+            pltpu.VMEM((n, 48, rows), F32),
+            pltpu.VMEM((48, rows), F32),
+            pltpu.VMEM((4, 48, rows), F32),
+            pltpu.VMEM((192, rows), F32),
+            pltpu.VMEM((rows, 192), F32),
+            pltpu.VMEM((SLOTS, width, BLOCK), BF),
+            pltpu.VMEM((SLOTS, width, BLOCK), BF),
+            pltpu.VMEM((SLOTS, BLOCK, width), BF),
+            pltpu.VMEM((n, 2, 2, tr, f), BF),
+            pltpu.VMEM((n, 2, 2, tr, f), BF),
+            pltpu.VMEM((n, 2, tr, f), BF),
+            pltpu.VMEM((n, 2, tr, f), BF),
+            pltpu.VMEM((n - 1, 2, tr, f), BF),
+            pltpu.VMEM((n - 1, 2, tr, f), BF),
+            pltpu.VMEM((2, tr, f), F32),
+            dma((3, SLOTS)),
+        ]
+        + [dma((2, n))] * 8
+        + [dma((n,))] * 2 + [dma((4,))] * 2 + [dma((n,))] * 6,
+        compiler_params=pltpu.CompilerParams(
+            collective_id=0, has_side_effects=True, vmem_limit_bytes=63 * 2**20
+        ),
+        cost_estimate=pl.CostEstimate(
+            flops=12 * rows * width * units, bytes_accessed=6 * width * units, transcendentals=0
+        ),
+    )(tokens, cotangent, gates, at, bd, bins, adt,
+      gate_weight_frozen, up_weight_frozen, down_weight_frozen)
+    ein = jnp.swapaxes(ein.reshape(4, 2, 16, piece), 2, 3)
+    return (
+        mixed, grad, ein, eout.reshape(1, 2, 16, units), din.T[None],
+        dout.reshape(4, 16, piece),
+    )
+
+
+def fits(mesh):
+    return mesh.shape["expert"] == 4 and mesh.shape["tensor"] == 4
+
+
 def solution(mesh):
     in_specs = (
         P(("group", "expert"), "tensor"),
@@ -272,4 +634,5 @@
         P(("group", "expert"), "tensor", None),
         P("group", None, ("expert", "tensor")),
     )
-    return jax.shard_map(local, mesh=mesh, in_specs=in_specs, out_specs=out_specs, check_vma=False)
+    step = fused if fits(mesh) else local
+    return jax.shard_map(step, mesh=mesh, in_specs=in_specs, out_specs=out_specs, check_vma=False)

time: 404 us -> 125 us (0.31)
  waiting for transfers between devices: 167 us -> 0 us
  Pallas kernels: 0 us -> 110 us
  matrix products: 107 us -> 0 us
  blocking collectives: 60.6 us -> 0 us
  starting transfers between devices: 20.8 us -> 0 us
  local copies, waits for them, and re-layouts: 26.6 us -> 9.47 us
  between operations: 14.2 us -> 0.64 us
  other arithmetic: 6.47 us -> 2.03 us
    reduce_scatter x4 -> x0, waiting for transfers between devices: 142 us -> none  [the longest x1 69.9 us: local(): lax.psum_scatter(table_a_in, ('expert', 'tensor'), scatter_dimension=2, t...]
    pallas_call x0 -> x1, Pallas kernels: none -> 110 us  [fused(): pl.pallas_call(functools.partial(fused_kernel, n), out_shape=(sds((tr, f)...]
    dot_general x29 -> x0, matrix products: 107 us -> none  [the longest x1 14.5 us: expert_forward_step(): jnp.dot(gate_gradient, gate_weight_slices.T, preferred_element_type=jnp.f...]
    all_gather x4 -> x0, blocking collectives: 60.6 us -> none  [the longest x1 15.7 us: local(): lax.all_gather(tokens, 'tensor', axis=1, tiled=True)]
    all_to_all x5 -> x0, waiting for transfers between devices: 25.7 us -> none  [the longest x1 22.2 us: local(): lax.all_to_all(input_gradient, 'expert', split_axis=0, concat_axis=0, til...]
    all_to_all x5 -> x0, starting transfers between devices: 20.6 us -> none  [the longest x1 4.51 us: local(): lax.all_to_all(weighted, 'expert', split_axis=0, concat_axis=0, tiled=True)]
    reshape x6 -> x0, local copies, waits for them, and re-layouts: 12.5 us -> none  [the longest x2 5.49 us: collect_rows(): jnp.sum(back.reshape(expert_number, copy_count, capacity, row_width), axi...]
    unnamed x62 -> x6, local copies, waits for them, and re-layouts: 5.07 us -> 9.47 us
  transfers between devices with their start and end apart: 9 -> 0, of which waited for: 5 -> 0; matrix products, arithmetic and copies ran while one was open for 20% -> 0% of each run, Pallas kernels for 0% -> 0%
where the time goes in v1:
time: 125 us; the launch traced here: 123 us
  Pallas kernels  110 us (88%)
  local copies, waits for them, and re-layouts  9.47 us (8%)
  other arithmetic  2.03 us (2%)
    pallas_call x1, Pallas kernels, fused(): pl.pallas_call(functools.partial(fused_kernel, n), out_shape=(sds((tr, f)...  110 us
    unnamed x6, local copies, waits for them, and re-layouts  9.47 us

profile of v1, /device:TPU:0, one launch (start us, length us, event | category | flops | bytes accessed | tf_op | source)
XLA Modules:
  0.0 122.6 jit_solution(78827917994020956)
XLA Ops:
  0.6 0.7 convert_element_type.3
  1.3 1.4 %select_reduce_fusion.gates_ref = f32[32,64]{1,0:T(8,128)} fusion(f32[32,2]{0,1:T(2,128)S(1)} %convert_element_type.3, s32[32,2]{0,1:T(2,128)} %param.12), kind=kLoop, calls=%fused_computation | loop fusion | flops 10240 | bytes 8704 | tf_op jit(solution)/shard_map/reduce_sum | solution.py:544
  2.7 110.5 %shard_map.154 = (bf16[32,1536]{1,0:T(8,128)(2,1)}, bf16[32,1536]{1,0:T(8,128)(2,1)}, f32[128,384]{1,0:T(8,128)}, f32[32,2048]{1,0:T(8,128)}, f32[16,2048]{1,0:T(8,128)}, /*index=5*/f32[64,384]{1,0:T(8,128)}) custom-call(bf16[32,1536]{1,0:T(8,128)(2,1)} %tok_ref.1, bf16[32,1536]{1,0:T(8,128)(2,1)} %cot_ref.1, f32[32,64]{1,0:T(8,128)} %select_reduce_fusion.gates_ref, ...), custom_call_target="tpu_custom_call" | custom-call | flops 19327352832 | bytes 75497472 | tf_op jit(solution)/shard_map/pallas_call | solution.py:561
  113.2 1.5 %copy.25 = bf16[32,1536]{1,0:T(8,128)(2,1)} copy(bf16[32,1536]{1,0:T(8,128)(2,1)} %get-tuple-element.24) | data formatting | bytes 196608
  114.7 1.5 %copy.26 = bf16[32,1536]{1,0:T(8,128)(2,1)} copy(bf16[32,1536]{1,0:T(8,128)(2,1)} %get-tuple-element.25) | data formatting | bytes 196608
  116.2 1.6 %copy.27 = f32[4,2,384,16]{2,3,1,0:T(8,128)} copy(f32[4,2,384,16]{2,3,1,0:T(8,128)} %bitcast.19) | data formatting | bytes 393216
  117.8 1.7 %copy.28 = f32[1,2,16,2048]{3,2,1,0:T(8,128)} copy(f32[1,2,16,2048]{3,2,1,0:T(8,128)} %bitcast.17) | data formatting | bytes 524288
  119.5 1.6 %copy.29 = f32[1,2048,16]{1,2,0:T(8,128)} copy(f32[1,2048,16]{1,2,0:T(8,128)} %bitcast.21) | data formatting | bytes 262144
  121.1 1.5 %copy.30 = f32[4,16,384]{2,1,0:T(8,128)} copy(f32[4,16,384]{2,1,0:T(8,128)} %bitcast.22) | data formatting | bytes 196608

commit v2 on v1

--- a/solution.py
+++ b/solution.py
@@ -275,9 +275,9 @@
 
 def fused_kernel(
     n_tensor,
-    tok_ref, cot_ref, gates_ref, at_ref, bd_ref, bin_ref, adt_ref, wg_ref, wu_ref, wd_ref,
+    tok_ref, cot_ref, route_ref, weight_ref, at_ref, bd_ref, bin_ref, adt_ref, wg_ref, wu_ref, wd_ref,
     mixed_ref, grad_ref, ein_ref, eout_ref, din_ref, dout_ref,
-    xy, small, gmat, sel_ref, selt_ref, acc, tacc, tz, ts, te, tvz, tvzt,
+    xy, small, gmat, sel_ref, selt_ref, acc, acct, tacc, tz, ts, te, tvz, tvzt,
     wg_buf, wu_buf, wd_buf, s1, r1, s2, r2, s3, r3, keep,
     wsem, gz_s, gz_r, gx_s, gx_r, gs_s, gs_r, gf_s, gf_r,
     tz_s, tz_r, te_s, te_r, c1_s, c1_r, c2_s, c2_r, c3_s, c3_r,
@@ -286,7 +286,7 @@
     t = lax.axis_index("tensor")
     n = n_tensor
     tr, f = tok_ref.shape
-    rows, width = gmat.shape
+    width, rows = gmat.shape
     units = adt_ref.shape[1]
     blocks = units // BLOCK
     xi, ci = e // 2, e % 2
@@ -375,7 +375,11 @@
 
     low = dot_nt(tok_ref[...], at_ref[...])
     yb = dot_nt(cot_ref[...], bd_ref[...])
-    gd = gates_ref[...]
+    label = lax.broadcasted_iota(jnp.int32, (tr, 64), 1)
+    routes, weights = route_ref[...], weight_ref[...].astype(F32)
+    gd = jnp.zeros((tr, 64), F32)
+    for j in range(routes.shape[1]):
+        gd = gd + jnp.where(label == routes[:, j : j + 1], weights[:, j : j + 1], 0.0)
     rank = bd_ref.shape[0] // 4
     lane = lax.broadcasted_iota(jnp.int32, yb.shape, 1) // rank
     scale = jnp.zeros_like(yb)
@@ -417,8 +421,9 @@
     gcol = picked[:, 48:49]
     for q in range(n):
         c = slice(q * f, (q + 1) * f)
-        gmat[:, c] = (gcol * xy[1, :, c].astype(F32)).astype(BF)
-    acc[...] = jnp.zeros_like(acc)
+        gmat[c, :] = (gcol * xy[1, :, c].astype(F32)).T.astype(BF)
+    acc[0] = jnp.zeros_like(acc[0])
+    acct[...] = jnp.zeros_like(acct)
     tacc[...] = jnp.zeros_like(tacc)
 
     def body(j, carry):
@@ -436,12 +441,14 @@
         x = xy[0]
         p = dot_nn(x, wg_buf[slot]) + adapter_scale * dot_nn(l0, bin0)
         u = dot_nn(x, wu_buf[slot]) + adapter_scale * dot_nn(l1, bin1)
-        ee = dot_nt(gmat[...], wd_buf[slot]) + adapter_scale * dot_nn(qn, adt)
+        ee = dot_nn(wd_buf[slot], gmat[...]).T + adapter_scale * dot_nn(qn, adt)
         sig = jax.nn.sigmoid(p)
         silu = p * sig
         h = (silu * u).astype(BF)
-        dg = (ee * u * sig * (1.0 + p * (1.0 - sig))).astype(BF)
-        du = (ee * silu).astype(BF)
+        dgf = ee * u * sig * (1.0 + p * (1.0 - sig))
+        duf = ee * silu
+        dg, du = dgf.astype(BF), duf.astype(BF)
+        dgt, dut = dgf.T.astype(BF), duf.T.astype(BF)
         eout_ref[0:16, cols] = adapter_scale * dot_nn(selt[0:16], dg)
         eout_ref[16:32, cols] = adapter_scale * dot_nn(selt[16:32], du)
         din_ref[:, cols] = adapter_scale * dot_nn(selt[32:48], h)
@@ -451,7 +458,7 @@
         for q in range(n):
             c = slice(q * f, (q + 1) * f)
             acc[0, :, c] += dot_nn(h, wd_buf[slot, :, c])
-            acc[1, :, c] += dot_nt(dg, wg_buf[slot, c, :]) + dot_nt(du, wu_buf[slot, c, :])
+            acct[c, :] += dot_nn(wg_buf[slot, c, :], dgt) + dot_nn(wu_buf[slot, c, :], dut)
 
         @pl.when(j + SLOTS < blocks)
         def _():
@@ -461,6 +468,9 @@
         return carry
 
     lax.fori_loop(0, blocks, body, 0)
+    for q in range(n):
+        c = slice(q * f, (q + 1) * f)
+        acc[1, :, c] = acct[c, :].T
 
     def mine(a, o, q):
         v = acc[a, row_ds(o), col_ds(q)]
@@ -531,6 +541,11 @@
         copy.wait_send()
 
 
+def store_results(*refs):
+    for source, target in zip(refs[:6], refs[6:]):
+        target[...] = source[...]
+
+
 def fused(
     tokens, route_experts, route_weight_values, cotangent,
     gate_weight_frozen, up_weight_frozen, down_weight_frozen,
@@ -540,15 +555,6 @@
     tr, f = tokens.shape
     width, rows = f * n, tr * 4
     units = down_weight_frozen.shape[1]
-    labels = jnp.arange(64, dtype=jnp.int32)
-    gates = jnp.sum(
-        jnp.where(
-            route_experts[:, :, None] == labels[None, None, :],
-            route_weight_values.astype(F32)[:, :, None],
-            0.0,
-        ),
-        axis=1,
-    )
     at = jnp.swapaxes(entry_input_maps, 2, 3).reshape(128, f)
     bd = down_output_maps.reshape(64, f)
     bins = entry_output_maps.reshape(32, units)
@@ -558,21 +564,23 @@
     anym = pl.BlockSpec(memory_space=pl.ANY)
     sds = jax.ShapeDtypeStruct
     dma = pltpu.SemaphoreType.DMA
-    mixed, grad, ein, eout, din, dout = pl.pallas_call(
-        functools.partial(fused_kernel, n),
-        out_shape=(
+    shapes = (
             sds((tr, f), BF), sds((tr, f), BF), sds((128, piece), F32),
             sds((32, units), F32), sds((16, units), F32), sds((64, piece), F32),
-        ),
-        in_specs=[vm] * 7 + [anym] * 3,
+    )
+    results = pl.pallas_call(
+        functools.partial(fused_kernel, n),
+        out_shape=shapes,
+        in_specs=[vm] * 8 + [anym] * 3,
         out_specs=(vm,) * 6,
         scratch_shapes=[
             pltpu.VMEM((2, rows, width), BF),
             pltpu.VMEM((n, rows, 256), F32),
-            pltpu.VMEM((rows, width), BF),
+            pltpu.VMEM((width, rows), BF),
             pltpu.VMEM((rows, 128), F32),
             pltpu.VMEM((128, rows), F32),
             pltpu.VMEM((2, rows, width), F32),
+            pltpu.VMEM((width, rows), F32),
             pltpu.VMEM((48, rows), F32),
             pltpu.VMEM((n, 48, rows), F32),
             pltpu.VMEM((48, rows), F32),
@@ -599,8 +607,11 @@
         cost_estimate=pl.CostEstimate(
             flops=12 * rows * width * units, bytes_accessed=6 * width * units, transcendentals=0
         ),
-    )(tokens, cotangent, gates, at, bd, bins, adt,
+    )(tokens, cotangent, route_experts, route_weight_values, at, bd, bins, adt,
       gate_weight_frozen, up_weight_frozen, down_weight_frozen)
+    mixed, grad, ein, eout, din, dout = pl.pallas_call(
+        store_results, out_shape=shapes, in_specs=[vm] * 6, out_specs=(vm,) * 6
+    )(*results)
     ein = jnp.swapaxes(ein.reshape(4, 2, 16, piece), 2, 3)
     return (
         mixed, grad, ein, eout.reshape(1, 2, 16, units), din.T[None],

time: 125 us -> 106 us (0.85)
  Pallas kernels: 110 us -> 100 us
  local copies, waits for them, and re-layouts: 9.47 us -> 2.7 us
  other arithmetic: 2.03 us -> 0 us
    pallas_call x1 -> x2, Pallas kernels: 110 us -> 100 us  [the longest x1 98.2 us: fused(): pl.pallas_call(functools.partial(fused_kernel, n), out_shape=shapes, in_s...]
    unnamed x6 -> x2, local copies, waits for them, and re-layouts: 9.47 us -> 2.7 us
    reduce_sum x1 -> x0, other arithmetic: 1.37 us -> none  [fused(): jnp.sum(jnp.where(route_experts[:, :, None] == labels[None, None, :], rou...]
where the time goes in v2:
time: 106 us; the launch traced here: 104 us
  Pallas kernels  100 us (94%)
  local copies, waits for them, and re-layouts  2.7 us (3%)
    pallas_call x1, Pallas kernels, fused(): pl.pallas_call(functools.partial(fused_kernel, n), out_shape=shapes, in_s...  98.2 us
    unnamed x2, local copies, waits for them, and re-layouts  2.7 us

profile of v2, /device:TPU:0, one launch (start us, length us, event | category | flops | bytes accessed | tf_op | source)
XLA Modules:
  0.0 103.7 jit_solution(15293778036139019988)
XLA Ops:
  0.6 1.3 %copy.18.weight_ref = bf16[32,2]{1,0:T(8,128)(2,1)} copy(bf16[32,2]{0,1:T(2,128)(2,1)} %param.13) | data formatting | bytes 256 | tf_op args[2]
  2.0 1.4 %copy.17.route_ref = s32[32,2]{1,0:T(8,128)} copy(s32[32,2]{0,1:T(2,128)} %param.12) | data formatting | bytes 512 | tf_op args[1]
  3.3 98.2 %shard_map.154 = (bf16[32,1536]{1,0:T(8,128)(2,1)}, bf16[32,1536]{1,0:T(8,128)(2,1)}, f32[128,384]{1,0:T(8,128)}, f32[32,2048]{1,0:T(8,128)}, f32[16,2048]{1,0:T(8,128)}, /*index=5*/f32[64,384]{1,0:T(8,128)}) custom-call(bf16[32,1536]{1,0:T(8,128)(2,1)} %tok_ref.1, bf16[32,1536]{1,0:T(8,128)(2,1)} %cot_ref.1, s32[32,2]{1,0:T(8,128)} %copy.17.route_ref, ...), custom_call_target="tpu_custom_call" | custom-call | flops 19327352832 | bytes 75497472 | tf_op jit(solution)/shard_map/pallas_call | solution.py:571
  101.6 2.1 %shard_map.155 = (bf16[32,1536]{1,0:T(8,128)(2,1)}, bf16[32,1536]{1,0:T(8,128)(2,1)}, f32[128,384]{1,0:T(8,128)}, f32[32,2048]{1,0:T(8,128)}, f32[16,2048]{1,0:T(8,128)}, /*index=5*/f32[64,384]{1,0:T(8,128)}) custom-call(bf16[32,1536]{1,0:T(8,128)(2,1)} %get-tuple-element.18.refs_0_, bf16[32,1536]{1,0:T(8,128)(2,1)} %get-tuple-element.19.refs_1_, ...), custom_call_target="tpu_custom_call" | custom-call | tf_op jit(solution)/shard_map/pallas_call | solution.py:612
